TPU v7x, 512 devices: a whole 4x4x16 slice. The times are simulated.
512 devices in a mesh: band: 8 (over x, core), pw: 64 (over z, y).
Axes of the slice: x: 4, y: 4, z: 16, core: 2. Of those that a mesh axis runs over, the one named last changes fastest.
Arguments:
- orbital_coefficients: float32 [8, 2, 128, 128, 128], P('band', None, 'pw'), may hold values from -6 to 6
- sphere_halfwidth: int32 [128, 128], P('pw'), may hold values from -1 to 63, as said below
- occupation: float32 [8], P('band'), may hold values from 0.5 to 2
- local_potential: float32 [256, 256, 256], P(None, 'pw'), may hold values from -6 to 6
- stencil_corner: int32 [64, 64, 128], P('pw'), may hold values from 0 to 262143, as said below
- stencil_weight: float32 [8, 64, 64, 128], P(None, 'pw'), may hold values from -3 to 3
- point_count: int32 [64, 64], P('pw'), may hold values from 0 to 128, as said below
Outputs:
- local_action: float32 [8, 2, 128, 128, 128], P('band', None, 'pw')
- fit_potential: float32 [64, 64, 128], P('pw')
Inputs may be any that keep to these rules, and one draw needn't show every extreme that they name: `sphere_halfwidth`: in every draw the kept columns form one sphere centred at frequency zero that reaches the cube's faces; -1 marks an empty column. `stencil_corner`: each corner is x * 4 + y times 256 plus z, with x and z in 0 to 255 and y in 0 to 3. `point_count`: in every draw some tile has all 128 slots live from every source, and every source has some block with all 128 slots live.
All inputs are finite; a program needn't handle non-finite values.
Results may differ from a plain program's by a relative error of at most 0.0003.
Values sent between devices are 32-bit elements; how exact they have to be, the bound alone decides.
A program may use at most 64 MiB of HBM per device.

v0:
```python
import math
import jax
import jax.numpy as jnp
from jax import lax
from jax.sharding import PartitionSpec as P

hartree_scale = 200.0
exact_mode = lax.Precision.HIGHEST


def shifted(value, axis, steps):
    count = lax.axis_size(axis)
    pairs = [(source, (source + steps) % count) for source in range(count)]
    return lax.ppermute(value, axis, pairs)


def phases(frequency, grid_size):
    position = jnp.arange(grid_size, dtype=jnp.int32)
    product = jnp.remainder(frequency[:, None] * position[None, :], grid_size)
    angle = product.astype(jnp.float32) * (2.0 * math.pi / grid_size)
    return (jnp.cos(angle), jnp.sin(angle))


def inverse_table(frequency, grid_size):
    cosine, sine = phases(frequency, grid_size)
    from_real = jnp.stack([cosine, sine], axis=1)
    from_imag = jnp.stack([-sine, cosine], axis=1)
    return jnp.stack([from_real, from_imag], axis=0)


def forward_table(frequency, grid_size):
    cosine, sine = phases(frequency, grid_size)
    from_real = jnp.stack([cosine.T, -sine.T], axis=1)
    from_imag = jnp.stack([sine.T, cosine.T], axis=1)
    return jnp.stack([from_real, from_imag], axis=0)


def transform(operand, matrix, target_axis, component_axis):
    result = lax.dot_general(
        operand,
        matrix,
        (((component_axis, target_axis), (0, 1)), ((), ())),
        precision=exact_mode,
        preferred_element_type=jnp.float32,
    )
    dimensions = operand.ndim
    return jnp.moveaxis(result, (dimensions - 2, dimensions - 1), (component_axis, target_axis))


def kernel_values(start_x, count_x, start_y, count_y, grid_size):

    def signed(start, count):
        frequency = start + jnp.arange(count, dtype=jnp.int32)
        return jnp.where(frequency < grid_size // 2, frequency, frequency - grid_size)

    along_x = signed(start_x, count_x)
    along_y = signed(start_y, count_y)
    along_z = signed(0, grid_size)
    square = along_x[:, None, None] ** 2 + along_y[None, :, None] ** 2 + along_z[None, None, :] ** 2
    return jnp.where(square > 0, hartree_scale / jnp.maximum(square, 1).astype(jnp.float32), 0.0)


def body(
    orbital_coefficients,
    sphere_halfwidth,
    occupation,
    local_potential,
    stencil_corner,
    stencil_weight,
    point_count,
):
    cube_size = orbital_coefficients.shape[3]
    grid_size = local_potential.shape[0]
    slab_depth = local_potential.shape[1]
    slot_count = stencil_corner.shape[2]
    cube_freq = jnp.arange(cube_size, dtype=jnp.int32) - cube_size // 2
    sphere_mask = (jnp.abs(cube_freq)[None, None, :] <= sphere_halfwidth[:, :, None]).astype(
        jnp.float32
    )
    scale_in = float(cube_size) ** (-1.5)
    scale_out = float(cube_size) ** 1.5 / float(grid_size) ** 3
    inverse_cube = inverse_table(cube_freq, grid_size)
    forward_cube = forward_table(cube_freq, grid_size)
    coefficient = orbital_coefficients * (sphere_mask * scale_in)[None, None]
    partial_section = transform(coefficient, inverse_cube, 4, 1)
    partial_section = transform(partial_section, inverse_cube, 3, 1)
    orbital = transform(
        lax.all_to_all(partial_section, "pw", split_axis=3, concat_axis=2, tiled=True),
        inverse_cube,
        2,
        1,
    )
    partial_density = jnp.sum(
        occupation[:, None, None, None] * (orbital[:, 0] ** 2 + orbital[:, 1] ** 2), axis=0
    )
    product = orbital * local_potential[None, None]
    forward_section = transform(product, forward_cube, 2, 1)
    pencil = lax.all_to_all(forward_section, "pw", split_axis=2, concat_axis=3, tiled=True)
    pencil = transform(pencil, forward_cube, 3, 1)
    spectrum_cube = transform(pencil, forward_cube, 4, 1)
    local_action = spectrum_cube * (sphere_mask * scale_out)[None, None]
    grid_freq = jnp.arange(grid_size, dtype=jnp.int32)
    forward_grid = forward_table(grid_freq, grid_size)
    inverse_grid = inverse_table(grid_freq, grid_size)
    pw_count = lax.axis_size("pw")
    band_count = lax.axis_size("band")
    x_block = grid_size // pw_count
    x_start = lax.axis_index("pw") * x_block
    inverse_norm = 1.0 / float(grid_size) ** 3
    y_block = grid_size // band_count
    y_start = lax.axis_index("band") * y_block
    density_part = lax.psum_scatter(partial_density, "band", scatter_dimension=2, tiled=True)
    spectrum = transform(density_part[None], forward_grid[0:1], 1, 0)
    spectrum = lax.all_to_all(spectrum, "pw", split_axis=1, concat_axis=2, tiled=True)
    spectrum = transform(spectrum, forward_grid, 2, 0)
    spectrum = lax.all_to_all(spectrum, "band", split_axis=2, concat_axis=3, tiled=True)
    spectrum = transform(spectrum, forward_grid, 3, 0)
    spectrum = spectrum * kernel_values(x_start, x_block, y_start, y_block, grid_size)[None]
    spectrum = transform(spectrum, inverse_grid, 3, 0)
    spectrum = lax.all_to_all(spectrum, "band", split_axis=3, concat_axis=2, tiled=True)
    spectrum = transform(spectrum, inverse_grid, 2, 0)
    spectrum = lax.all_to_all(spectrum, "pw", split_axis=2, concat_axis=1, tiled=True)
    hartree_part = transform(spectrum, inverse_grid[:, :, 0:1], 1, 0)[0] * inverse_norm
    hartree = lax.all_gather(hartree_part, "band", axis=2, tiled=True)
    upper_plane = shifted(hartree[:, 0:1, :], "pw", -1)
    extended = jnp.concatenate([hartree, upper_plane], axis=1)
    flattened = extended.reshape(-1)
    plane_cells = slab_depth * grid_size
    request = lax.all_to_all(stencil_corner, "pw", split_axis=1, concat_axis=0, tiled=True)
    coord_x = request // plane_cells
    coord_y = request // grid_size % slab_depth
    coord_z = request % grid_size
    gathered = []
    for corner in range(8):
        step_x = corner // 4
        step_y = corner // 2 % 2
        step_z = corner % 2
        cell_index = (
            (coord_x + step_x) % grid_size * (slab_depth + 1) + coord_y + step_y
        ) * grid_size + (coord_z + step_z) % grid_size
        gathered.append(flattened[cell_index])
    stacked = jnp.stack(gathered, axis=0)
    sampled = lax.all_to_all(stacked, "pw", split_axis=1, concat_axis=2, tiled=True)
    summed = jnp.sum(stencil_weight * sampled, axis=0)
    live_slot = jnp.arange(slot_count, dtype=jnp.int32)[None, None, :] < point_count[:, :, None]
    fit_potential = jnp.where(live_slot, summed, 0.0)
    return (local_action, fit_potential)


def solution(mesh):
    placed = (
        P("band", None, "pw", None, None),
        P("pw", None),
        P("band"),
        P(None, "pw", None),
        P("pw", None, None),
        P(None, "pw", None, None),
        P("pw", None),
    )
    return jax.shard_map(
        body,
        mesh=mesh,
        in_specs=placed,
        out_specs=(P("band", None, "pw", None, None), P("pw", None, None)),
        check_vma=False,
    )
```

profile of v0, /device:TPU:8, one launch (start us, length us, event | category | flops | bytes accessed | tf_op | source)
XLA Modules:
  0.0 736.5 jit_solution(2443056056476492475)
XLA Ops:
  11.6 18.7 %all-to-all-start = ((f32[1,2,2,256,256]{4,1,2,0,3:T(2,128)}), f32[1,2,2,256,256]{4,1,2,0,3:T(2,128)S(1)}, u32[]{:S(2)}, u32[]{:S(2)}) async-start(f32[1,2,2,256,256]{4,1,2,0,3:T(2,128)} %copy.52), calls=%async_computation | async-start | bytes 2097152 | tf_op jit(solution)/shard_map/all_to_all | solution.py:88
  31.1 54.5 %all-to-all-done = f32[1,2,2,256,256]{4,1,2,0,3:T(2,128)S(1)} async-done(((f32[1,2,2,256,256]{4,1,2,0,3:T(2,128)}), f32[1,2,2,256,256]{4,1,2,0,3:T(2,128)S(1)}, u32[]{:S(2)}, u32[]{:S(2)}) %all-to-all-start) | async-done | bytes 1048608 | tf_op jit(solution)/shard_map/all_to_all | solution.py:88
  91.4 29.4 %reduce-scatter.2.cloned.1.call-done = f32[256,4,32]{0,2,1:T(8,128)} async-done(((f32[256,4,256]{0,2,1:T(8,128)}), f32[256,4,32]{0,2,1:T(8,128)}) %reduce-scatter.2.cloned.1.call-update) | async-done | bytes 131088 | tf_op jit(solution)/shard_map/reduce_scatter | solution.py:112
  125.6 16.2 %all-to-all-start.2 = ((f32[64,1,1024]{2,1,0:T(1,128)}), f32[64,1,1024]{2,1,0:T(1,128)}, u32[]{:S(2)}, u32[]{:S(2)}) async-start(f32[64,1,1024]{2,1,0:T(1,128)} %reshape.1541), calls=%async_computation.3 | async-start | bytes 524288 | tf_op jit(solution)/shard_map/all_to_all | solution.py:114
  145.5 15.2 %all-to-all-done.2 = f32[64,1,1024]{2,1,0:T(1,128)} async-done(((f32[64,1,1024]{2,1,0:T(1,128)}), f32[64,1,1024]{2,1,0:T(1,128)}, u32[]{:S(2)}, u32[]{:S(2)}) %all-to-all-start.2) | async-done | bytes 262176 | tf_op jit(solution)/shard_map/all_to_all | solution.py:114
  170.8 3.0 reshape.1543
  173.8 4.5 all-to-all-start.3
  179.2 6.9 all-to-all-done.3
  190.1 2.8 copy.151
  198.4 2.3 reshape.1545
  200.7 10.6 %all_to_all.126 = f32[8,1,8192]{2,1,0:T(1,128)} all-to-all(f32[8,1,8192]{2,1,0:T(1,128)S(1)} %reshape.1545), channel_id=1, replica_groups=mesh['band'=8,'pw'=64] {'band'}, dimensions={0} | all-to-all | bytes 524288 | tf_op jit(solution)/shard_map/all_to_all | solution.py:120
  211.3 6.1 all-to-all-start.6
  221.6 2.8 copy.150
  231.0 14.9 %all-to-all-start.5 = ((f32[64,1,1024]{2,1,0:T(1,128)}), f32[64,1,1024]{2,1,0:T(1,128)S(1)}, u32[]{:S(2)}, u32[]{:S(2)}) async-start(f32[64,1,1024]{2,1,0:T(1,128)} %reshape.1547), calls=%async_computation.6 | async-start | bytes 524288 | tf_op jit(solution)/shard_map/all_to_all | solution.py:122
  248.8 2.8 fusion.3
  251.6 2.3 copy.58
  253.8 12.9 %all-to-all-done.5 = f32[64,1,1024]{2,1,0:T(1,128)S(1)} async-done(((f32[64,1,1024]{2,1,0:T(1,128)}), f32[64,1,1024]{2,1,0:T(1,128)S(1)}, u32[]{:S(2)}, u32[]{:S(2)}) %all-to-all-start.5) | async-done | bytes 262176 | tf_op jit(solution)/shard_map/all_to_all | solution.py:122
  266.7 6.2 all-to-all-start.1
  276.9 2.4 fusion.11
  279.3 30.2 %all-gather.3.cloned.1.call-done = f32[1,256,4,256]{1,3,2,0:T(8,128)} async-done(((f32[1,256,4,32]{1,3,2,0:T(8,128)}), f32[1,256,4,256]{1,3,2,0:T(8,128)}) %all-gather.3.cloned.1.call-update) | async-done | bytes 1048592 | tf_op jit(solution)/shard_map/all_gather | solution.py:124
  310.5 2.4 collective-permute-start
  315.9 6.3 collective-permute-done
  324.9 45.7 %gather_fusion.7 = f32[8192]{0:T(1024)S(1)} fusion(f32[327680]{0:T(1024)S(1)} %reshape.1420, s32[8192]{0:T(1024)} %get-tuple-element.8), kind=kCustom, calls=%fused_computation.7 | custom fusion | bytes 98304 | tf_op jit(solution)/shard_map/gather | solution.py:141
  370.6 45.5 %gather_fusion.6 = f32[8192]{0:T(1024)S(1)} fusion(f32[327680]{0:T(1024)S(1)} %reshape.1420, s32[8192]{0:T(1024)S(1)} %copy-done.18), kind=kCustom, calls=%fused_computation.6 | custom fusion | bytes 98304 | tf_op jit(solution)/shard_map/gather | solution.py:141
  416.2 45.5 %gather_fusion.5 = f32[8192]{0:T(1024)S(1)} fusion(f32[327680]{0:T(1024)S(1)} %reshape.1420, s32[8192]{0:T(1024)S(1)} %copy-done.17), kind=kCustom, calls=%fused_computation.5 | custom fusion | bytes 98304 | tf_op jit(solution)/shard_map/gather | solution.py:141
  461.7 45.5 %gather_fusion.4 = f32[8192]{0:T(1024)S(1)} fusion(f32[327680]{0:T(1024)S(1)} %reshape.1420, s32[8192]{0:T(1024)S(1)} %copy-done.16), kind=kCustom, calls=%fused_computation.4 | custom fusion | bytes 98304 | tf_op jit(solution)/shard_map/gather | solution.py:141
  507.3 45.5 %gather_fusion.3 = f32[8192]{0:T(1024)S(1)} fusion(f32[327680]{0:T(1024)S(1)} %reshape.1420, s32[8192]{0:T(1024)S(1)} %copy-done.12), kind=kCustom, calls=%fused_computation.3 | custom fusion | bytes 98304 | tf_op jit(solution)/shard_map/gather | solution.py:141
  552.9 45.5 %gather_fusion.2 = f32[8192]{0:T(1024)S(1)} fusion(f32[327680]{0:T(1024)S(1)} %reshape.1420, s32[8192]{0:T(1024)S(1)} %copy-done.15), kind=kCustom, calls=%fused_computation.2 | custom fusion | bytes 98304 | tf_op jit(solution)/shard_map/gather | solution.py:141
  598.4 45.5 %gather_fusion.1 = f32[8192]{0:T(1024)S(1)} fusion(f32[327680]{0:T(1024)S(1)} %reshape.1420, s32[8192]{0:T(1024)S(1)} %copy-done.14), kind=kCustom, calls=%fused_computation.1 | custom fusion | bytes 98304 | tf_op jit(solution)/shard_map/gather | solution.py:141
  644.0 45.5 %gather_fusion = f32[8192]{0:T(1024)S(1)} fusion(f32[327680]{0:T(1024)S(1)} %reshape.1420, s32[8192]{0:T(1024)S(1)} %copy-done.13), kind=kCustom, calls=%fused_computation | custom fusion | bytes 98304 | tf_op jit(solution)/shard_map/gather | solution.py:141
  690.6 16.6 %all-to-all-start.7 = ((f32[8,64,1,128]{3,0,2,1:T(8,128)}), f32[8,64,1,128]{3,0,2,1:T(8,128)S(1)}, u32[]{:S(2)}, u32[]{:S(2)}) async-start(f32[8,64,1,128]{3,0,2,1:T(8,128)} %stack.131), calls=%async_computation.8 | async-start | bytes 524288 | tf_op jit(solution)/shard_map/all_to_all | solution.py:143
  713.3 15.0 %all-to-all-done.7 = f32[8,64,1,128]{3,0,2,1:T(8,128)S(1)} async-done(((f32[8,64,1,128]{3,0,2,1:T(8,128)}), f32[8,64,1,128]{3,0,2,1:T(8,128)S(1)}, u32[]{:S(2)}, u32[]{:S(2)}) %all-to-all-start.7) | async-done | bytes 262176 | tf_op jit(solution)/shard_map/all_to_all | solution.py:143
  (111 shorter events, 71.4 us)
Async XLA Ops:
  7.2 1.5 copy-start.11
  11.6 73.9 %all-to-all-start = ((f32[1,2,2,256,256]{4,1,2,0,3:T(2,128)}), f32[1,2,2,256,256]{4,1,2,0,3:T(2,128)S(1)}, u32[]{:S(2)}, u32[]{:S(2)}) async-start(f32[1,2,2,256,256]{4,1,2,0,3:T(2,128)} %copy.52), calls=%async_computation | async-start | bytes 2097152 | tf_op jit(solution)/shard_map/all_to_all | solution.py:88
  30.4 90.4 %reduce-scatter.2.cloned.1.call-start = ((), (), s32[]{:S(2)}) async-start(), calls=%async_computation.9 | async-start | bytes 1179648 | tf_op jit(solution)/shard_map/reduce_scatter | solution.py:112
  91.4 29.4 %copy-start.9 = (f32[256,1,256]{2,0,1:T(8,128)}, f32[256,1,256]{2,0,1:T(8,128)S(1)}, u32[]{:S(2)}) copy-start(f32[256,1,256]{2,0,1:T(8,128)S(1)} %fusion.57) | copy-start | bytes 786436
  125.6 35.1 %all-to-all-start.2 = ((f32[64,1,1024]{2,1,0:T(1,128)}), f32[64,1,1024]{2,1,0:T(1,128)}, u32[]{:S(2)}, u32[]{:S(2)}) async-start(f32[64,1,1024]{2,1,0:T(1,128)} %reshape.1541), calls=%async_computation.3 | async-start | bytes 524288 | tf_op jit(solution)/shard_map/all_to_all | solution.py:114
  144.0 1.3 copy-start.1
  144.1 1.4 copy-start.3
  166.4 1.2 copy-start
  173.8 12.2 %all-to-all-start.3 = ((f32[8,1,8192]{2,1,0:T(1,128)}), f32[8,1,8192]{2,1,0:T(1,128)}, u32[]{:S(2)}, u32[]{:S(2)}) async-start(f32[8,1,8192]{2,1,0:T(1,128)} %reshape.1543), calls=%async_computation.4 | async-start | bytes 524288 | tf_op jit(solution)/shard_map/all_to_all | solution.py:116
  211.3 19.6 %all-to-all-start.6 = ((s32[1,64,128]{2,0,1:T(1,128)}), s32[1,64,128]{2,0,1:T(1,128)}, u32[]{:S(2)}, u32[]{:S(2)}) async-start(s32[1,64,128]{2,0,1:T(1,128)} %bitcast.297), calls=%async_computation.7 | async-start | bytes 65536 | tf_op jit(solution)/shard_map/all_to_all | solution.py:129
  231.0 35.8 %all-to-all-start.5 = ((f32[64,1,1024]{2,1,0:T(1,128)}), f32[64,1,1024]{2,1,0:T(1,128)S(1)}, u32[]{:S(2)}, u32[]{:S(2)}) async-start(f32[64,1,1024]{2,1,0:T(1,128)} %reshape.1547), calls=%async_computation.6 | async-start | bytes 524288 | tf_op jit(solution)/shard_map/all_to_all | solution.py:122
  248.0 0.7 copy-start.5
  248.0 0.8 copy-start.7
  266.7 423.9 %all-to-all-start.1 = ((f32[1,2,128,4,256]{4,1,3,0,2:T(2,128)}), f32[1,2,128,4,256]{4,1,3,0,2:T(2,128)}, u32[]{:S(2)}, u32[]{:S(2)}) async-start(f32[1,2,128,4,256]{4,1,3,0,2:T(2,128)} %copy.58), calls=%async_computation.1 | async-start | bytes 2097152 | tf_op jit(solution)/shard_map/all_to_all | solution.py:98
  273.0 36.5 %all-gather.3.cloned.1.call-start = ((), (), s32[]{:S(2)}) async-start(), calls=%async_computation.10 | async-start | bytes 1179648 | tf_op jit(solution)/shard_map/all_gather | solution.py:124
  275.7 1.0 copy-start.2
  275.7 1.2 copy-start.4
  310.5 11.8 %collective-permute-start = (f32[256,1,256]{0,2,1:T(8,128)S(1)}, f32[256,1,256]{0,2,1:T(8,128)S(1)}, u32[]{:S(2)}, u32[]{:S(2)}) collective-permute-start(f32[256,1,256]{0,2,1:T(8,128)S(1)} %slice.36), channel_id=1, source_target_pairs={{0,63},{1,0},{2,1},{3,2},{4,3},{5,4},{6,5},{7,6},{8,7},{9,8},{10,9... | collective-permute-start | bytes 786440 | tf_op jit(solution)/shard_map/ppermute | solution.py:14
  324.9 45.7 %copy-start.18 = (s32[8192]{0:T(1024)S(1)}, s32[8192]{0:T(1024)}, u32[]{:S(2)}) copy-start(s32[8192]{0:T(1024)} %get-tuple-element.22) | copy-start | bytes 98308
  370.6 45.6 %copy-start.17 = (s32[8192]{0:T(1024)S(1)}, s32[8192]{0:T(1024)}, u32[]{:S(2)}) copy-start(s32[8192]{0:T(1024)} %get-tuple-element.23) | copy-start | bytes 98308
  416.2 45.6 %copy-start.16 = (s32[8192]{0:T(1024)S(1)}, s32[8192]{0:T(1024)}, u32[]{:S(2)}) copy-start(s32[8192]{0:T(1024)} %get-tuple-element.24) | copy-start | bytes 98308
  461.7 45.6 %copy-start.12 = (s32[8192]{0:T(1024)S(1)}, s32[8192]{0:T(1024)}, u32[]{:S(2)}) copy-start(s32[8192]{0:T(1024)} %get-tuple-element.31) | copy-start | bytes 98308
  507.3 45.6 %copy-start.15 = (s32[8192]{0:T(1024)S(1)}, s32[8192]{0:T(1024)}, u32[]{:S(2)}) copy-start(s32[8192]{0:T(1024)} %get-tuple-element.30) | copy-start | bytes 98308
  552.8 45.6 %copy-start.14 = (s32[8192]{0:T(1024)S(1)}, s32[8192]{0:T(1024)}, u32[]{:S(2)}) copy-start(s32[8192]{0:T(1024)} %get-tuple-element.29) | copy-start | bytes 98308
  598.4 45.6 %copy-start.13 = (s32[8192]{0:T(1024)S(1)}, s32[8192]{0:T(1024)}, u32[]{:S(2)}) copy-start(s32[8192]{0:T(1024)} %get-tuple-element.28) | copy-start | bytes 98308
  690.6 37.7 %all-to-all-start.7 = ((f32[8,64,1,128]{3,0,2,1:T(8,128)}), f32[8,64,1,128]{3,0,2,1:T(8,128)S(1)}, u32[]{:S(2)}, u32[]{:S(2)}) async-start(f32[8,64,1,128]{3,0,2,1:T(8,128)} %stack.131), calls=%async_computation.8 | async-start | bytes 524288 | tf_op jit(solution)/shard_map/all_to_all | solution.py:143
  708.7 1.0 copy-start.6
  708.7 1.0 copy-start.8
  711.5 16.8 %copy-start.10 = (f32[8,1,64,128]{3,2,1,0:T(8,128)S(1)}, f32[8,1,64,128]{3,2,1,0:T(8,128)}, u32[]{:S(2)}) copy-start(f32[8,1,64,128]{3,2,1,0:T(8,128)} %param.12) | copy-start | bytes 786436
  711.5 17.0 %copy-start.19 = (s32[1,64]{1,0:T(1,128)S(1)}, s32[1,64]{1,0:T(1,128)}, u32[]{:S(2)}) copy-start(s32[1,64]{1,0:T(1,128)} %param.13) | copy-start | bytes 772
Sparse Core Ops, SparseCore 0:
  89.5 31.1 reduce-scatter.1
  279.4 29.9 all-gather.2
where the time goes:
time: 746 us; the launch traced here: 737 us
  local copies, waits for them, and re-layouts  411 us (55%)
  waiting for transfers between devices  170 us (23%)
  starting transfers between devices  86.1 us (12%)
  other arithmetic  22.6 us (3%)
  matrix products  19.7 us (3%)
  between operations  15.8 us (2%)
  blocking collectives  10.6 us (1%)
    gather x8, local copies, waits for them, and re-layouts, body(): gathered.append(flattened[cell_index])  364 us
    all_to_all x1, waiting for transfers between devices, body(): lax.all_to_all(partial_section, 'pw', split_axis=3, concat_axis=2, tiled=...  54.5 us
    all_gather x1, waiting for transfers between devices, body(): hartree = lax.all_gather(hartree_part, 'band', axis=2, tiled=True)  30.2 us
    reduce_scatter x1, waiting for transfers between devices, body(): lax.psum_scatter(partial_density, 'band', scatter_dimension=2, tiled=True)  29.4 us
    dot_general x12, matrix products, transform(): lax.dot_general(operand, matrix, (((component_axis, target_axis), (0, 1))...  19.7 us
    unnamed x50, local copies, waits for them, and re-layouts  19.3 us
    all_to_all x1, starting transfers between devices, body(): lax.all_to_all(partial_section, 'pw', split_axis=3, concat_axis=2, tiled=...  18.7 us
    all_to_all x1, starting transfers between devices, body(): lax.all_to_all(stacked, 'pw', split_axis=1, concat_axis=2, tiled=True)  16.6 us
  transfers between devices with their start and end apart: 10, of which 9 were waited for; matrix products, arithmetic and copies ran while one was open for 56% of the time, Pallas kernels for 0%

commit v1 on v0

--- a/solution.py
+++ b/solution.py
@@ -121,7 +121,9 @@
     spectrum = transform(spectrum, inverse_grid, 2, 0)
     spectrum = lax.all_to_all(spectrum, "pw", split_axis=2, concat_axis=1, tiled=True)
     hartree_part = transform(spectrum, inverse_grid[:, :, 0:1], 1, 0)[0] * inverse_norm
-    hartree = lax.all_gather(hartree_part, "band", axis=2, tiled=True)
+    hartree = jnp.concatenate(
+        lax.all_to_all(jnp.stack([hartree_part] * lax.axis_size("band")), "band", 0, 0), axis=2
+    )
     upper_plane = shifted(hartree[:, 0:1, :], "pw", -1)
     extended = jnp.concatenate([hartree, upper_plane], axis=1)
     flattened = extended.reshape(-1)

time: 746 us -> 773 us (1.036)
  the two profiles are of different devices: /device:TPU:8 before, /device:TPU:2 now
where the time goes in v1:
time: 773 us; the launch traced here: 764 us
  local copies, waits for them, and re-layouts  414 us (54%)
  waiting for transfers between devices  176 us (23%)
  starting transfers between devices  80.7 us (10%)
  blocking collectives  38.5 us (5%)
  other arithmetic  20 us (3%)
  matrix products  19 us (2%)
  between operations  15.7 us (2%)
    gather x8, local copies, waits for them, and re-layouts, body(): gathered.append(flattened[cell_index])  364 us
    all_to_all x1, waiting for transfers between devices, body(): lax.all_to_all(partial_section, 'pw', split_axis=3, concat_axis=2, tiled=...  54.6 us
    ppermute x1, waiting for transfers between devices, shifted(): return lax.ppermute(value, axis, pairs)  40.7 us
    all_to_all x1, blocking collectives, body(): lax.all_to_all(spectrum, 'pw', split_axis=2, concat_axis=1, tiled=True)  27.7 us
    reduce_scatter x1, waiting for transfers between devices, body(): lax.psum_scatter(partial_density, 'band', scatter_dimension=2, tiled=True)  26.1 us
    unnamed x38, local copies, waits for them, and re-layouts  19.4 us
    dot_general x12, matrix products, transform(): lax.dot_general(operand, matrix, (((component_axis, target_axis), (0, 1))...  19 us
    all_to_all x1, starting transfers between devices, body(): lax.all_to_all(partial_section, 'pw', split_axis=3, concat_axis=2, tiled=...  18.7 us
  transfers between devices with their start and end apart: 9, of which 8 were waited for; matrix products, arithmetic and copies ran while one was open for 52% of the time, Pallas kernels for 0%

profile of v1, /device:TPU:2, one launch (start us, length us, event | category | flops | bytes accessed | tf_op | source)
XLA Modules:
  0.0 763.7 jit_solution(1429343301351390845)
XLA Ops:
  11.6 18.7 %all-to-all-start = ((f32[1,2,2,256,256]{4,1,2,0,3:T(2,128)}), f32[1,2,2,256,256]{4,1,2,0,3:T(2,128)S(1)}, u32[]{:S(2)}, u32[]{:S(2)}) async-start(f32[1,2,2,256,256]{4,1,2,0,3:T(2,128)} %copy.53), calls=%async_computation | async-start | bytes 2097152 | tf_op jit(solution)/shard_map/all_to_all | solution.py:88
  31.1 54.6 %all-to-all-done = f32[1,2,2,256,256]{4,1,2,0,3:T(2,128)S(1)} async-done(((f32[1,2,2,256,256]{4,1,2,0,3:T(2,128)}), f32[1,2,2,256,256]{4,1,2,0,3:T(2,128)S(1)}, u32[]{:S(2)}, u32[]{:S(2)}) %all-to-all-start) | async-done | bytes 1048608 | tf_op jit(solution)/shard_map/all_to_all | solution.py:88
  91.5 26.1 %reduce-scatter.2.cloned.1.call-done = f32[256,4,32]{0,2,1:T(8,128)} async-done(((f32[256,4,256]{0,2,1:T(8,128)}), f32[256,4,32]{0,2,1:T(8,128)}) %reduce-scatter.2.cloned.1.call-update) | async-done | bytes 131088 | tf_op jit(solution)/shard_map/reduce_scatter | solution.py:112
  122.5 16.1 %all-to-all-start.2 = ((f32[64,1,1024]{2,1,0:T(1,128)}), f32[64,1,1024]{2,1,0:T(1,128)}, u32[]{:S(2)}, u32[]{:S(2)}) async-start(f32[64,1,1024]{2,1,0:T(1,128)} %reshape.1547), calls=%async_computation.3 | async-start | bytes 524288 | tf_op jit(solution)/shard_map/all_to_all | solution.py:114
  142.2 18.2 %all-to-all-done.2 = f32[64,1,1024]{2,1,0:T(1,128)} async-done(((f32[64,1,1024]{2,1,0:T(1,128)}), f32[64,1,1024]{2,1,0:T(1,128)}, u32[]{:S(2)}, u32[]{:S(2)}) %all-to-all-start.2) | async-done | bytes 262176 | tf_op jit(solution)/shard_map/all_to_all | solution.py:114
  170.6 3.0 reshape.1549
  173.6 5.7 all-to-all-start.3
  180.1 5.4 all-to-all-done.3
  189.6 2.8 copy.153
  200.2 10.8 %all_to_all.131 = f32[8,1,8192]{2,1,0:T(1,128)} all-to-all(f32[8,1,8192]{2,1,0:T(1,128)S(1)} %reshape.1551), channel_id=1, replica_groups=mesh['band'=8,'pw'=64] {'band'}, dimensions={0} | all-to-all | bytes 524288 | tf_op jit(solution)/shard_map/all_to_all | solution.py:120
  215.1 2.8 copy.152
  223.6 27.7 %all_to_all.132 = f32[64,1,1024]{2,1,0:T(1,128)S(1)} all-to-all(f32[64,1,1024]{2,1,0:T(1,128)S(1)} %reshape.1553), channel_id=1, replica_groups=mesh['band'=8,'pw'=64] {'pw'}, dimensions={0} | all-to-all | bytes 524288 | tf_op jit(solution)/shard_map/all_to_all | solution.py:122
  251.2 5.4 all-to-all-start.7
  262.1 8.9 %all-to-all-done.7 = s32[1,64,128]{2,0,1:T(1,128)} async-done(((s32[1,64,128]{2,0,1:T(1,128)}), s32[1,64,128]{2,0,1:T(1,128)}, u32[]{:S(2)}, u32[]{:S(2)}) %all-to-all-start.7) | async-done | bytes 32800 | tf_op jit(solution)/shard_map/all_to_all | solution.py:131
  272.1 5.2 all-to-all-start.6
  277.3 2.5 copy.57
  281.2 2.8 fusion.3
  284.0 2.3 copy.59
  286.3 5.5 all-to-all-done.6
  291.8 6.4 all-to-all-start.1
  298.3 7.0 collective-permute-start
  307.1 40.7 %collective-permute-done = f32[256,1,256]{0,2,1:T(8,128)S(1)} collective-permute-done((f32[256,1,256]{0,2,1:T(8,128)S(1)}, f32[256,1,256]{0,2,1:T(8,128)S(1)}, u32[]{:S(2)}, u32[]{:S(2)}) %collective-permute-start) | collective-permute-done | bytes 262176 | tf_op jit(solution)/shard_map/ppermute | solution.py:14
  351.5 45.5 %gather_fusion.7 = f32[8192]{0:T(1024)S(1)} fusion(f32[327680]{0:T(1024)S(1)} %reshape.1427, s32[8192]{0:T(1024)S(1)} %get-tuple-element.8), kind=kCustom, calls=%fused_computation.7 | custom fusion | bytes 98304 | tf_op jit(solution)/shard_map/gather | solution.py:143
  397.0 45.5 %gather_fusion.6 = f32[8192]{0:T(1024)S(1)} fusion(f32[327680]{0:T(1024)S(1)} %reshape.1427, s32[8192]{0:T(1024)S(1)} %get-tuple-element.22), kind=kCustom, calls=%fused_computation.6 | custom fusion | bytes 98304 | tf_op jit(solution)/shard_map/gather | solution.py:143
  442.5 45.5 %gather_fusion.5 = f32[8192]{0:T(1024)S(1)} fusion(f32[327680]{0:T(1024)S(1)} %reshape.1427, s32[8192]{0:T(1024)S(1)} %get-tuple-element.23), kind=kCustom, calls=%fused_computation.5 | custom fusion | bytes 98304 | tf_op jit(solution)/shard_map/gather | solution.py:143
  488.1 45.5 %gather_fusion.4 = f32[8192]{0:T(1024)S(1)} fusion(f32[327680]{0:T(1024)S(1)} %reshape.1427, s32[8192]{0:T(1024)S(1)} %get-tuple-element.24), kind=kCustom, calls=%fused_computation.4 | custom fusion | bytes 98304 | tf_op jit(solution)/shard_map/gather | solution.py:143
  533.6 45.5 %gather_fusion.3 = f32[8192]{0:T(1024)S(1)} fusion(f32[327680]{0:T(1024)S(1)} %reshape.1427, s32[8192]{0:T(1024)S(1)} %get-tuple-element.31), kind=kCustom, calls=%fused_computation.3 | custom fusion | bytes 98304 | tf_op jit(solution)/shard_map/gather | solution.py:143
  579.2 45.5 %gather_fusion.2 = f32[8192]{0:T(1024)S(1)} fusion(f32[327680]{0:T(1024)S(1)} %reshape.1427, s32[8192]{0:T(1024)S(1)} %get-tuple-element.30), kind=kCustom, calls=%fused_computation.2 | custom fusion | bytes 98304 | tf_op jit(solution)/shard_map/gather | solution.py:143
  624.7 45.5 %gather_fusion.1 = f32[8192]{0:T(1024)S(1)} fusion(f32[327680]{0:T(1024)S(1)} %reshape.1427, s32[8192]{0:T(1024)S(1)} %get-tuple-element.29), kind=kCustom, calls=%fused_computation.1 | custom fusion | bytes 98304 | tf_op jit(solution)/shard_map/gather | solution.py:143
  670.3 45.5 %gather_fusion = f32[8192]{0:T(1024)S(1)} fusion(f32[327680]{0:T(1024)S(1)} %reshape.1427, s32[8192]{0:T(1024)S(1)} %get-tuple-element.28), kind=kCustom, calls=%fused_computation | custom fusion | bytes 98304 | tf_op jit(solution)/shard_map/gather | solution.py:143
  716.9 16.1 %all-to-all-start.8 = ((f32[8,64,1,128]{3,0,2,1:T(8,128)}), f32[8,64,1,128]{3,0,2,1:T(8,128)S(1)}, u32[]{:S(2)}, u32[]{:S(2)}) async-start(f32[8,64,1,128]{3,0,2,1:T(8,128)} %stack.146), calls=%async_computation.9 | async-start | bytes 524288 | tf_op jit(solution)/shard_map/all_to_all | solution.py:145
  739.1 16.3 %all-to-all-done.8 = f32[8,64,1,128]{3,0,2,1:T(8,128)S(1)} async-done(((f32[8,64,1,128]{3,0,2,1:T(8,128)}), f32[8,64,1,128]{3,0,2,1:T(8,128)S(1)}, u32[]{:S(2)}, u32[]{:S(2)}) %all-to-all-start.8) | async-done | bytes 262176 | tf_op jit(solution)/shard_map/all_to_all | solution.py:145
  (99 shorter events, 72.4 us)
Async XLA Ops:
  7.2 1.5 copy-start.12
  11.6 74.0 %all-to-all-start = ((f32[1,2,2,256,256]{4,1,2,0,3:T(2,128)}), f32[1,2,2,256,256]{4,1,2,0,3:T(2,128)S(1)}, u32[]{:S(2)}, u32[]{:S(2)}) async-start(f32[1,2,2,256,256]{4,1,2,0,3:T(2,128)} %copy.53), calls=%async_computation | async-start | bytes 2097152 | tf_op jit(solution)/shard_map/all_to_all | solution.py:88
  30.4 87.3 %reduce-scatter.2.cloned.1.call-start = ((), (), s32[]{:S(2)}) async-start(), calls=%async_computation.10 | async-start | bytes 1179648 | tf_op jit(solution)/shard_map/reduce_scatter | solution.py:112
  91.5 26.2 %copy-start.10 = (f32[256,1,256]{2,0,1:T(8,128)}, f32[256,1,256]{2,0,1:T(8,128)S(1)}, u32[]{:S(2)}) copy-start(f32[256,1,256]{2,0,1:T(8,128)S(1)} %fusion.57) | copy-start | bytes 786436
  122.5 38.0 %all-to-all-start.2 = ((f32[64,1,1024]{2,1,0:T(1,128)}), f32[64,1,1024]{2,1,0:T(1,128)}, u32[]{:S(2)}, u32[]{:S(2)}) async-start(f32[64,1,1024]{2,1,0:T(1,128)} %reshape.1547), calls=%async_computation.3 | async-start | bytes 524288 | tf_op jit(solution)/shard_map/all_to_all | solution.py:114
  140.9 1.3 copy-start.1
  140.9 1.3 copy-start.3
  166.1 1.2 copy-start
  173.6 11.9 %all-to-all-start.3 = ((f32[8,1,8192]{2,1,0:T(1,128)}), f32[8,1,8192]{2,1,0:T(1,128)}, u32[]{:S(2)}, u32[]{:S(2)}) async-start(f32[8,1,8192]{2,1,0:T(1,128)} %reshape.1549), calls=%async_computation.4 | async-start | bytes 524288 | tf_op jit(solution)/shard_map/all_to_all | solution.py:116
  251.2 19.8 %all-to-all-start.7 = ((s32[1,64,128]{2,0,1:T(1,128)}), s32[1,64,128]{2,0,1:T(1,128)}, u32[]{:S(2)}, u32[]{:S(2)}) async-start(s32[1,64,128]{2,0,1:T(1,128)} %bitcast.301), calls=%async_computation.8 | async-start | bytes 65536 | tf_op jit(solution)/shard_map/all_to_all | solution.py:131
  259.1 1.0 copy-start.2
  259.1 1.2 copy-start.4
  272.1 19.7 %all-to-all-start.6 = ((f32[8,256,4,32]{1,3,2,0:T(8,128)}), f32[8,256,4,32]{1,3,2,0:T(8,128)S(1)}, u32[]{:S(2)}, u32[]{:S(2)}) async-start(f32[8,256,4,32]{1,3,2,0:T(8,128)} %stack.137), calls=%async_computation.7 | async-start | bytes 2097152 | tf_op jit(solution)/shard_map/all_to_all | solution.py:125
  279.9 1.4 copy-start.5
  280.4 0.7 copy-start.6
  280.4 0.8 copy-start.8
  291.8 425.1 %all-to-all-start.1 = ((f32[1,2,128,4,256]{4,1,3,0,2:T(2,128)}), f32[1,2,128,4,256]{4,1,3,0,2:T(2,128)}, u32[]{:S(2)}, u32[]{:S(2)}) async-start(f32[1,2,128,4,256]{4,1,3,0,2:T(2,128)} %copy.59), calls=%async_computation.1 | async-start | bytes 2097152 | tf_op jit(solution)/shard_map/all_to_all | solution.py:98
  298.3 49.5 %collective-permute-start = (f32[256,1,256]{0,2,1:T(8,128)S(1)}, f32[256,1,256]{0,2,1:T(8,128)S(1)}, u32[]{:S(2)}, u32[]{:S(2)}) collective-permute-start(f32[256,1,256]{0,2,1:T(8,128)S(1)} %slice.36), channel_id=1, source_target_pairs={{0,63},{1,0},{2,1},{3,2},{4,3},{5,4},{6,5},{7,6},{8,7},{9,8},{10,9... | collective-permute-start | bytes 786440 | tf_op jit(solution)/shard_map/ppermute | solution.py:14
  716.9 38.5 %all-to-all-start.8 = ((f32[8,64,1,128]{3,0,2,1:T(8,128)}), f32[8,64,1,128]{3,0,2,1:T(8,128)S(1)}, u32[]{:S(2)}, u32[]{:S(2)}) async-start(f32[8,64,1,128]{3,0,2,1:T(8,128)} %stack.146), calls=%async_computation.9 | async-start | bytes 524288 | tf_op jit(solution)/shard_map/all_to_all | solution.py:145
  734.5 1.0 copy-start.7
  734.5 1.0 copy-start.9
  737.3 18.1 %copy-start.11 = (f32[8,1,64,128]{3,2,1,0:T(8,128)S(1)}, f32[8,1,64,128]{3,2,1,0:T(8,128)}, u32[]{:S(2)}) copy-start(f32[8,1,64,128]{3,2,1,0:T(8,128)} %param.12) | copy-start | bytes 786436
  737.3 18.3 %copy-start.13 = (s32[1,64]{1,0:T(1,128)S(1)}, s32[1,64]{1,0:T(1,128)}, u32[]{:S(2)}) copy-start(s32[1,64]{1,0:T(1,128)} %param.13) | copy-start | bytes 772
Sparse Core Ops, SparseCore 0:
  89.7 27.9 reduce-scatter.1
